TPU v7x, 512 devices: a whole 4x8x8 slice. The times are simulated.
512 devices in a mesh: cuts: 32 (over x, z_hi, core), chip: 16 (over y, z_lo).
Axes of the slice: x: 4, y: 8, z: 8 (z_hi: 4, z_lo: 2; z = z_hi * 2 + z_lo), core: 2. Of those that a mesh axis runs over, the one named last changes fastest.
Arguments:
- hidden: bfloat16 [65536, 5120], P(('cuts', 'chip')), may hold values from -8 to 8
- out_grad: bfloat16 [65536, 5120], P(('cuts', 'chip')), may hold values from -24 to 24
- weights: bfloat16 [4, 5120, 128], P(None, 'chip'), may hold values from -0.078125 to 0.078125
Outputs:
- input_grad: bfloat16 [65536, 5120], P(('cuts', 'chip'))
- weight_grads: float32 [4, 5120, 128], P(None, ('cuts', 'chip'))
All inputs are finite; a program needn't handle non-finite values.
Results may differ from a plain program's by a relative error of at most 0.039.
Values may be sent and summed in bfloat16 or wider, within the bound.
A program may use at most 64 MiB of HBM per device.

v0:
```python
import jax
import jax.numpy as jnp
from jax import lax
from jax.sharding import PartitionSpec as P


def rope_tables(length, width):
    half = width // 2
    position = jnp.arange(length, dtype=jnp.float32)[:, None]
    rates = 10000.0 ** (-(jnp.arange(half, dtype=jnp.float32) * 2.0) / width)
    angle = position * rates[None, :]
    return (jnp.cos(angle), jnp.sin(angle))


def rotate(values, cosine, sine, flip):
    half = values.shape[1] // 2
    first = values[:, :half]
    second = values[:, half:]
    sine = sine * flip
    return jnp.concatenate([first * cosine - second * sine, second * cosine + first * sine], axis=1)


def local(hidden, out_grad, weights):
    full = lax.all_gather(weights, "chip", axis=1, tiled=True)
    w_out = full[3]
    w_qkv = full[:3]
    length, width = (hidden.shape[0], w_out.shape[1])
    model = w_out.shape[0]
    cosine, sine = rope_tables(length, width)
    scale = 1.0 / jnp.sqrt(jnp.float32(width))
    d_attn = jnp.dot(out_grad, w_out, preferred_element_type=jnp.float32).astype(jnp.bfloat16)
    query = rotate(
        jnp.dot(hidden, w_qkv[0], preferred_element_type=jnp.float32), cosine, sine, 1.0
    ).astype(jnp.bfloat16)
    keys = rotate(
        jnp.dot(hidden, w_qkv[1], preferred_element_type=jnp.float32), cosine, sine, 1.0
    ).astype(jnp.bfloat16)
    values = jnp.dot(hidden, w_qkv[2], preferred_element_type=jnp.float32).astype(jnp.bfloat16)
    scores = jnp.dot(query, keys.T, preferred_element_type=jnp.float32) * scale
    rows = jnp.arange(length)[:, None]
    cols = jnp.arange(length)[None, :]
    scores = jnp.where(cols <= rows, scores, -jnp.inf)
    top = jnp.max(scores, axis=1, keepdims=True)
    expo = jnp.exp(scores - top)
    prob = expo / jnp.sum(expo, axis=1, keepdims=True)
    prob_b = prob.astype(jnp.bfloat16)
    attn = jnp.dot(prob_b, values, preferred_element_type=jnp.float32).astype(jnp.bfloat16)
    d_prob = jnp.dot(d_attn, values.T, preferred_element_type=jnp.float32)
    d_score = (prob * (d_prob - jnp.sum(prob * d_prob, axis=1, keepdims=True)) * scale).astype(
        jnp.bfloat16
    )
    d_query = rotate(
        jnp.dot(d_score, keys, preferred_element_type=jnp.float32), cosine, sine, -1.0
    ).astype(jnp.bfloat16)
    d_key = rotate(
        jnp.dot(d_score.T, query, preferred_element_type=jnp.float32), cosine, sine, -1.0
    ).astype(jnp.bfloat16)
    d_value = jnp.dot(prob_b.T, d_attn, preferred_element_type=jnp.float32).astype(jnp.bfloat16)
    d_stack = jnp.stack([d_query, d_key, d_value])
    input_grad = jnp.einsum(
        "jte,jde->td", d_stack, w_qkv, preferred_element_type=jnp.float32
    ).astype(jnp.bfloat16)
    qkv_grads = jnp.einsum("td,jte->jde", hidden, d_stack, preferred_element_type=jnp.float32)
    out_grads = jnp.dot(out_grad.T, attn, preferred_element_type=jnp.float32)
    partial_value = jnp.concatenate([qkv_grads, out_grads[None]], axis=0).astype(jnp.bfloat16)
    cuts_count = lax.axis_size("cuts")
    chip_count = lax.axis_size("chip")
    owned = model // (cuts_count * chip_count)
    sectioned = partial_value.reshape(1, 4, cuts_count, chip_count, owned, width)
    received = lax.all_to_all(sectioned, "chip", split_axis=3, concat_axis=0, tiled=True)
    summed = jnp.sum(received.astype(jnp.float32), axis=0).reshape(1, 4, cuts_count, owned, width)
    received_two = lax.all_to_all(summed, "cuts", split_axis=2, concat_axis=0, tiled=True)
    total = jnp.sum(received_two, axis=0).reshape(4, owned, width)
    weight_grads = total / jnp.float32(cuts_count * chip_count)
    return (input_grad, weight_grads)


def solution(mesh):
    placed = (P(("cuts", "chip"), None), P(("cuts", "chip"), None), P(None, "chip", None))
    return jax.shard_map(
        local,
        mesh=mesh,
        in_specs=placed,
        out_specs=(P(("cuts", "chip"), None), P(None, ("cuts", "chip"), None)),
        check_vma=False,
    )
```

profile of v0, /device:TPU:6, one launch (start us, length us, event | category | flops | bytes accessed | tf_op | source)
XLA Modules:
  0.0 352.4 jit_solution(6045198130182369520)
XLA Ops:
  7.2 0.0 copy-start
  7.2 0.0 all-gather.2.cloned.1.call-start
  7.2 0.7 all-gather.2.cloned.1.call-update
  7.9 0.0 copy-start.9
  7.9 129.1 %all-gather.2.cloned.1.call-done = bf16[4,5120,128]{2,1,0:T(8,128)(2,1)} async-done(((bf16[4,320,128]{2,1,0:T(8,128)(2,1)}), bf16[4,5120,128]{2,1,0:T(8,128)(2,1)}) %all-gather.2.cloned.1.call-update) | async-done | bytes 5242896 | tf_op jit(solution)/shard_map/all_gather | solution.py:24
  137.0 0.0 copy-done
  137.0 2.1 fusion.7
  139.1 1.9 fusion.6
  141.1 0.0 copy-done.9
  141.1 0.2 subtract_convert_fusion.2
  141.3 0.2 fusion.33
  141.6 0.0 copy-done.1
  141.6 1.8 fusion.10
  143.4 0.8 fusion.12
  144.2 0.5 fusion.11
  144.7 0.2 multiply_reduce_fusion
  145.0 0.1 fusion.18
  145.1 0.2 fusion.19
  145.2 2.0 fusion.2
  147.3 1.6 copy.19
  148.9 2.4 concatenate.62
  151.3 0.9 fusion.23
  152.1 0.0 copy-start.2
  152.2 0.0 copy-start.4
  152.2 0.0 copy-start.6
  152.2 0.6 copy-done.2
  152.7 0.0 copy-done.4
  152.8 0.0 copy-done.6
  152.8 3.8 %fusion = bf16[3,5120,128]{1,2,0:T(8,128)(2,1)} fusion(bf16[128,5120]{1,0:T(8,128)(2,1)S(1)} %copy-done, bf16[1,128,128]{1,2,0:T(8,128)(2,1)} %fusion.12, bf16[1,128,64]{1,2,0:T(8,128)(2,1)S(1)} %get-tuple-element.10, bf16[1,128,64]{1,2,0:T(8,128)(2,1)S(1)} %get-tuple-element.11, bf16[1,128,64]{1,2,0:T(8,128)(2,1)S(1)} %get-tuple-element.3, ...), kind=kOutput, calls=%fused_computation.3 | convolution fusion | flops 505774080 | bytes 5341184 | tf_op jit(solution)/shard_map/td,jte->jde/dot_general | solution.py:63
  156.6 6.3 %copy.18 = bf16[3,5120,128]{2,1,0:T(8,128)(2,1)} copy(bf16[3,5120,128]{1,2,0:T(8,128)(2,1)} %fusion) | data formatting | bytes 7864320 | tf_op jit(solution)/shard_map/td,jte->jde/transpose | solution.py:63
  162.9 8.1 %concatenate.61 = bf16[1,3,32,16,10,128]{5,4,3,2,1,0:T(8,128)(2,1)} reshape(bf16[3,5120,128]{2,1,0:T(8,128)(2,1)} %copy.18) | data formatting | bytes 7864320 | tf_op jit(solution)/shard_map/concatenate | solution.py:65
  171.0 7.5 %pad_maximum_fusion = bf16[1,4,32,16,10,128]{5,4,3,2,1,0:T(8,128)(2,1)} fusion(bf16[1,1,32,16,10,128]{5,4,3,2,1,0:T(8,128)(2,1)S(1)} %concatenate.62, bf16[1,3,32,16,10,128]{5,4,3,2,1,0:T(8,128)(2,1)} %concatenate.61), kind=kLoop, calls=%fused_computation.1 | loop fusion | flops 2621440 | bytes 10485760 | tf_op jit(solution)/shard_map/concatenate | solution.py:65
  178.4 9.5 %copy.20 = bf16[1,4,32,16,10,128]{5,2,4,1,0,3:T(8,128)(2,1)S(1)} copy(bf16[1,4,32,16,10,128]{5,4,3,2,1,0:T(8,128)(2,1)} %pad_maximum_fusion) | data formatting | bytes 10485760 | tf_op jit(solution)/shard_map/concatenate | solution.py:65
  187.9 124.7 %all_to_all.8 = bf16[1,4,32,16,10,128]{5,2,4,1,0,3:T(8,128)(2,1)S(1)} all-to-all(bf16[1,4,32,16,10,128]{5,2,4,1,0,3:T(8,128)(2,1)S(1)} %copy.20), channel_id=1, replica_groups=mesh['cuts'=32,'chip'=16] {'chip'}, dimensions={3} | all-to-all | bytes 10485760 | tf_op jit(solution)/shard_map/all_to_all | solution.py:70
  312.6 0.9 convert_reduce_fusion
  313.5 0.0 copy-start.3
  313.5 0.0 copy-start.5
  313.5 0.0 copy-start.7
  313.6 0.0 copy-start.8
  313.6 1.3 copy.21
  314.8 10.7 %all-to-all-start.1 = ((f32[1,4,32,10,128]{4,1,3,0,2:T(4,128)}), f32[1,4,32,10,128]{4,1,3,0,2:T(4,128)S(1)}, u32[]{:S(2)}, u32[]{:S(2)}) async-start(f32[1,4,32,10,128]{4,1,3,0,2:T(4,128)} %copy.21), calls=%async_computation.1 | async-start | bytes 1310720 | tf_op jit(solution)/shard_map/all_to_all | solution.py:72
  325.6 0.0 copy-done.3
  325.6 0.0 copy-done.5
  325.6 0.0 copy-done.7
  325.6 4.6 %fusion.1 = bf16[128,5120]{1,0:T(8,128)(2,1)} fusion(bf16[4,5120,128]{2,1,0:T(8,128)(2,1)} %all-gather.2.cloned.1.call-done, bf16[1,128,128]{1,2,0:T(8,128)(2,1)S(1)} %copy-done.8, bf16[1,128,64]{1,2,0:T(8,128)(2,1)S(1)} %copy-done.5, bf16[1,128,64]{1,2,0:T(8,128)(2,1)S(1)} %copy-done.7, bf16[1,128,64]{1,2,0:T(8,128)(2,1)S(1)} %copy-done.3, ...), kind=kOutput, calls=%fused_computation.5 | convolution fusion | flops 504463360 | bytes 5341184 | tf_op jit(solution)/shard_map/jte,jde->td/dot_general | solution.py:60
  330.2 14.6 %all-to-all-done.1 = f32[1,4,32,10,128]{4,1,3,0,2:T(4,128)S(1)} async-done(((f32[1,4,32,10,128]{4,1,3,0,2:T(4,128)}), f32[1,4,32,10,128]{4,1,3,0,2:T(4,128)S(1)}, u32[]{:S(2)}, u32[]{:S(2)}) %all-to-all-start.1) | async-done | bytes 655392 | tf_op jit(solution)/shard_map/all_to_all | solution.py:72
  344.8 0.1 reduce_sum.39
  344.9 0.6 broadcast_multiply_fusion
  (5 shorter events, 0.1 us)
Async XLA Ops:
  7.2 129.9 %copy-start = (bf16[128,5120]{1,0:T(8,128)(2,1)S(1)}, bf16[128,5120]{1,0:T(8,128)(2,1)}, u32[]{:S(2)}) copy-start(bf16[128,5120]{1,0:T(8,128)(2,1)} %param.3) | copy-start | bytes 3932164
  7.2 129.8 %all-gather.2.cloned.1.call-start = ((), (), s32[]{:S(2)}) async-start(), calls=%async_computation.2 | async-start | bytes 5570560 | tf_op jit(solution)/shard_map/all_gather | solution.py:24
  7.9 133.1 %copy-start.9 = (f32[64]{0:T(128)}, f32[64]{0:T(128)S(1)}, u32[]{:S(2)}) copy-start(f32[64]{0:T(128)S(1)} %multiply_power_fusion) | copy-start | bytes 772
  137.0 4.5 %copy-start.1 = (bf16[4,5120,128]{2,1,0:T(8,128)(2,1)S(1)}, bf16[4,5120,128]{2,1,0:T(8,128)(2,1)}, u32[]{:S(2)}) copy-start(bf16[4,5120,128]{2,1,0:T(8,128)(2,1)} %all-gather.2.cloned.1.call-done) | copy-start | bytes 15728644
  152.1 0.6 copy-start.2
  152.2 0.6 copy-start.4
  152.2 0.6 copy-start.6
  313.5 12.0 %copy-start.3 = (bf16[1,128,64]{1,2,0:T(8,128)(2,1)S(1)}, bf16[1,128,64]{1,2,0:T(8,128)(2,1)}, u32[]{:S(2)}) copy-start(bf16[1,128,64]{1,2,0:T(8,128)(2,1)} %copy-done.2) | copy-start | bytes 49156
  313.5 12.0 %copy-start.5 = (bf16[1,128,64]{1,2,0:T(8,128)(2,1)S(1)}, bf16[1,128,64]{1,2,0:T(8,128)(2,1)}, u32[]{:S(2)}) copy-start(bf16[1,128,64]{1,2,0:T(8,128)(2,1)} %copy-done.4) | copy-start | bytes 49156
  313.5 12.0 %copy-start.7 = (bf16[1,128,64]{1,2,0:T(8,128)(2,1)S(1)}, bf16[1,128,64]{1,2,0:T(8,128)(2,1)}, u32[]{:S(2)}) copy-start(bf16[1,128,64]{1,2,0:T(8,128)(2,1)} %copy-done.6) | copy-start | bytes 49156
  313.6 12.0 %copy-start.8 = (bf16[1,128,128]{1,2,0:T(8,128)(2,1)S(1)}, bf16[1,128,128]{1,2,0:T(8,128)(2,1)}, u32[]{:S(2)}) copy-start(bf16[1,128,128]{1,2,0:T(8,128)(2,1)} %fusion.12) | copy-start | bytes 98308
  314.8 30.0 %all-to-all-start.1 = ((f32[1,4,32,10,128]{4,1,3,0,2:T(4,128)}), f32[1,4,32,10,128]{4,1,3,0,2:T(4,128)S(1)}, u32[]{:S(2)}, u32[]{:S(2)}) async-start(f32[1,4,32,10,128]{4,1,3,0,2:T(4,128)} %copy.21), calls=%async_computation.1 | async-start | bytes 1310720 | tf_op jit(solution)/shard_map/all_to_all | solution.py:72
Sparse Core Ops, SparseCore 0:
  10.1 126.8 all-gather.1
where the time goes:
time: 356 us; the launch traced here: 352 us
  waiting for transfers between devices  144 us (40%)
  blocking collectives  125 us (35%)
  local copies, waits for them, and re-layouts  29.7 us (8%)
  matrix products  18.3 us (5%)
  between operations  14.2 us (4%)
  starting transfers between devices  10.8 us (3%)
  other arithmetic  10.3 us (3%)
    all_gather x1, waiting for transfers between devices, local(): full = lax.all_gather(weights, 'chip', axis=1, tiled=True)  129 us
    all_to_all x1, blocking collectives, local(): lax.all_to_all(sectioned, 'chip', split_axis=3, concat_axis=0, tiled=True)  125 us
    concatenate x3, local copies, waits for them, and re-layouts, local(): jnp.concatenate([qkv_grads, out_grads[None]], axis=0).astype(jnp.bfloat16)  19.9 us
    all_to_all x1, waiting for transfers between devices, local(): lax.all_to_all(summed, 'cuts', split_axis=2, concat_axis=0, tiled=True)  14.6 us
    all_to_all x1, starting transfers between devices, local(): lax.all_to_all(summed, 'cuts', split_axis=2, concat_axis=0, tiled=True)  10.7 us
    concatenate x1, other arithmetic, local(): jnp.concatenate([qkv_grads, out_grads[None]], axis=0).astype(jnp.bfloat16)  7.48 us
  transfers between devices with their start and end apart: 2, of which 2 were waited for; matrix products, arithmetic and copies ran while one was open for 1% of the time, Pallas kernels for 0%

commit v1 on v0

v1 whole, which is shorter than its diff:
```python
import jax
import jax.numpy as jnp
import numpy as np
from jax import lax
from jax.experimental import pallas as pl
from jax.experimental.pallas import tpu as pltpu
from jax.sharding import PartitionSpec as P

MESH = pl.DeviceIdType.MESH
F32 = jnp.float32
BF16 = jnp.bfloat16

HD = 128
SEQ = 128
HALF = 2560
ITEM = 640
CHUNK = 1280
BLOCK = 160


def rope_tables():
    half = HD // 2
    rates = 10000.0 ** (-(np.arange(half) * 2.0) / HD)
    angle = np.arange(SEQ)[:, None] * rates[None, :]
    cosine, sine = np.cos(angle), np.sin(angle)
    return (
        np.concatenate([cosine, cosine], axis=1).astype(np.float32),
        np.concatenate([-sine, sine], axis=1).astype(np.float32),
    )


def dot(a, b):
    return jnp.dot(a, b, preferred_element_type=F32)


def dot_nt(a, b):
    return lax.dot_general(a, b, (((1,), (1,)), ((), ())), preferred_element_type=F32)


def kernel(
    hid, og, wts, cosr, sinr, ig_out, wg_out,
    Hb, Ob, W, HT, OT, acc, accr, DD, PP, Ropp, Rn, Ro, Sb, Rz, T, U, Ru, IG,
    loc_sem, sib_s, sib_r, g1_s, g1_r, g2_s, g2_r,
    opp_s, opp_r, nb_s, nb_r, own_s, own_r, z_s, z_r, y_s, y_r,
):
    ci = lax.axis_index("cuts")
    ch = lax.axis_index("chip")
    x = ci // 8
    zh = (ci // 2) % 4
    c = ci % 2
    y = ch // 2
    zl = ch % 2
    z = zh * 2 + zl
    o = 1 - c

    def dev(x_, y_, z_, c_):
        return (x_ * 8 + (z_ // 2) * 2 + c_, y_ * 2 + z_ % 2)

    def rcopy(src, dst, ss, rs, to):
        return pltpu.make_async_remote_copy(
            src_ref=src, dst_ref=dst, send_sem=ss, recv_sem=rs, device_id=to, device_id_type=MESH
        )

    sib = dev(x, y, z, o)
    active = y // 4 == c
    base = pl.multiple_of((y % 4) * ITEM + zl * 320, 32)
    base_o = pl.multiple_of((y % 4) * ITEM + (1 - zl) * 320, 32)
    mine = pl.ds(pl.multiple_of(c * SEQ, SEQ), SEQ)
    theirs = pl.ds(pl.multiple_of(o * SEQ, SEQ), SEQ)
    col_c = pl.ds(pl.multiple_of(c * HALF, HALF), HALF)
    col_o = pl.ds(pl.multiple_of(o * HALF, HALF), HALF)

    lh = pltpu.make_async_copy(hid.at[:, col_c], Hb.at[mine, :], loc_sem.at[0])
    lo = pltpu.make_async_copy(og.at[:, col_c], Ob.at[mine, :], loc_sem.at[1])
    lw = pltpu.make_async_copy(wts, W.at[:, pl.ds(base, 320), :], loc_sem.at[2])

    @pl.when(active)
    def _():
        lw.start()

    lh.start()
    lo.start()

    bar = pltpu.get_barrier_semaphore()

    def greet(to):
        pl.semaphore_signal(bar, inc=1, device_id=to, device_id_type=MESH)

    greet(sib)
    for dx in (1, 3):
        for cc in (0, 1):
            greet(dev((x + dx) % 4, y, z, cc))
    for dz in range(1, 8):
        greet(dev(x, y, (z + dz) % 8, c))
    for dy in range(1, 8):
        for l in (0, 1):
            greet(dev(x, (y + dy) % 8, zh * 2 + l, c))
    acc[...] = jnp.zeros_like(acc)
    T[...] = jnp.zeros_like(T)
    pl.semaphore_wait(bar, 1 + 4 + 7 + 14)

    zp, zm = (z + 1) % 8, (z + 7) % 8
    g1 = [
        rcopy(
            wts.at[:, pl.ds(160 * i, 160), :],
            W.at[:, pl.ds(base + 160 * i, 160), :],
            g1_s.at[i], g1_r.at[i], dev(x, y, (zp, zm)[i], c),
        )
        for i in range(2)
    ]

    @pl.when(active)
    def _():
        g1[0].start()
        g1[1].start()

    sh = rcopy(hid.at[:, col_o], Hb.at[mine, :], sib_s.at[0], sib_r.at[0], sib)
    so = rcopy(og.at[:, col_o], Ob.at[mine, :], sib_s.at[1], sib_r.at[1], sib)
    sh.start()
    so.start()

    yp, ym = (y + 1) % 8, (y + 7) % 8

    def item_ref(s, sub):
        return W.at[pl.ds(2 * sub, 2), pl.ds(pl.multiple_of((s % 4) * ITEM, 128), ITEM), :]

    def forward(s, t, d, sub):
        r = item_ref(s, sub)
        return rcopy(
            r, r, g2_s.at[t, d, sub], g2_r.at[s % 4, sub], dev(x, (yp, ym)[d], z, c)
        )

    def arrived(s, sub):
        r = item_ref(s, sub)
        rcopy(r, r, g2_s.at[0, 0, sub], g2_r.at[s % 4, sub], dev(x, yp, z, c)).wait_recv()

    def project(s):
        at = pl.ds(pl.multiple_of((s % 4) * ITEM, 128), ITEM)
        wq = jnp.concatenate([W[0, at, :], W[1, at, :], W[2, at, :]], axis=1)
        acc[:, 0:384] += dot(Hb[:, at], wq)
        acc[:, 384:512] += dot(Ob[:, at], W[3, at, :])

    def transpose(src, dst, q):
        turned = src[:, q * ITEM : (q + 1) * ITEM].T
        for i in range(4):
            zr, cr = (q % 2) * 2 + i // 2, i % 2
            at = (q // 2) * CHUNK + (cr * 4 + zr) * BLOCK
            dst[at : at + BLOCK, :] = turned[i * BLOCK : (i + 1) * BLOCK, :]

    @pl.when(active)
    def _():
        lw.wait()
        for i in range(2):
            rcopy(
                wts.at[:, pl.ds(160 * i, 160), :],
                W.at[:, pl.ds(base_o + 160 * i, 160), :],
                g1_s.at[i], g1_r.at[i], dev(x, y, (zp, zm)[i], c),
            ).wait_recv()
        for sub, d in ((0, 0), (1, 1), (1, 0), (0, 1)):
            forward(y, 0, d, sub).start()

    lh.wait()
    sh.wait_recv()
    for q in range(4):
        transpose(Hb, HT, q)
    lo.wait()
    so.wait_recv()

    @pl.when(active)
    def _():
        project(y)

    for t in range(1, 5):
        sources = ((y + 8 - t) % 8, (y + t) % 8)
        if t < 4:
            for sub in (0, 1):
                for d in (0, 1):
                    s = sources[d]
                    sb = sub if d == 0 else 1 - sub

                    @pl.when(s // 4 == c)
                    def _():
                        arrived(s, sb)
                        if t < 3 or sb == d:
                            forward(s, t, d, sb).start()

            if t == 1:
                for q in range(4):
                    transpose(Ob, OT, q)
            for d in (0, 1):
                s = sources[d]

                @pl.when(s // 4 == c)
                def _():
                    project(s)

        else:
            s = sources[0]

            @pl.when(s // 4 == c)
            def _():
                arrived(s, 0)
                arrived(s, 1)
                project(s)

    sa = rcopy(acc.at[theirs, :], accr, sib_s.at[2], sib_r.at[2], sib)
    sa.start()
    cosine, sine = cosr[...], sinr[...]

    def rope(v, sgn):
        return v * cosine + pltpu.roll(v, 64, 1) * (sine * sgn)

    scale = 1.0 / np.sqrt(np.float32(HD))
    rows = lax.broadcasted_iota(jnp.int32, (SEQ, SEQ), 0)
    cols = lax.broadcasted_iota(jnp.int32, (SEQ, SEQ), 1)
    sa.wait_recv()
    summed = acc[mine, :] + accr[...]
    query = rope(summed[:, 0:128], 1.0).astype(BF16)
    keys = rope(summed[:, 128:256], 1.0).astype(BF16)
    values = summed[:, 256:384].astype(BF16)
    d_attn = summed[:, 384:512].astype(BF16)
    scores = dot_nt(query, keys) * scale
    d_prob = dot_nt(d_attn, values)
    scores = jnp.where(cols <= rows, scores, -jnp.inf)
    expo = jnp.exp(scores - jnp.max(scores, axis=1, keepdims=True))
    prob = expo / jnp.sum(expo, axis=1, keepdims=True)
    prob_b = prob.astype(BF16)
    attn = dot(prob_b, values)
    d_score = prob * (d_prob - jnp.sum(prob * d_prob, axis=1, keepdims=True)) * scale
    d_query = rope(dot(d_score.astype(BF16), keys), -1.0)
    d_key = rope(dot(d_score.T.astype(BF16), query), -1.0)
    d_value = dot(prob.T.astype(BF16), d_attn)
    DD[mine, :] = jnp.concatenate([d_query, d_key, d_value, attn], axis=1).astype(BF16)
    sd = rcopy(DD.at[mine, :], DD.at[mine, :], sib_s.at[3], sib_r.at[3], sib)
    sd.start()
    rcopy(DD.at[theirs, :], DD.at[theirs, :], sib_s.at[3], sib_r.at[3], sib).wait_recv()

    dd = (2 * c + 4 - x) % 4
    is_opp = (dd == 1) | (dd == 2)
    plus = dd < 2
    kn = jnp.where((dd == 0) | (dd == 2), 1, 0)
    ks = 1 - kn
    xn = jnp.where(plus, (x + 1) % 4, (x + 3) % 4)
    xp, xm = (x + 1) % 4, (x + 3) % 4
    slot = jnp.where(plus, 0, 1)
    lane_f = pl.multiple_of(jnp.where(plus, 0, 256), 256)
    lane_d = pl.multiple_of(jnp.where(plus, 256, 0), 256)

    def piece(k, rb):
        at = pl.ds(pl.multiple_of(k * CHUNK + rb * BLOCK, 32), BLOCK)
        left = dot(HT[at, :], DD[:, 0:384])
        right = dot(OT[at, :], DD[:, 384:512])
        return at, left.astype(BF16), right.astype(BF16)

    def opp_copy(rb, h):
        return rcopy(
            PP.at[pl.ds(pl.multiple_of(ks * CHUNK + rb * BLOCK, 32), BLOCK), pl.ds(256 * h, 256)],
            Ropp.at[pl.ds(pl.multiple_of(rb * BLOCK, 32), BLOCK), :],
            opp_s.at[rb, h], opp_r.at[rb], dev((xp, xm)[h], y, z, c),
        )

    def nb_copy(rb, h, lane):
        cr, zr = rb // 4, rb % 4
        return rcopy(
            PP.at[pl.ds(pl.multiple_of(kn * CHUNK + rb * BLOCK, 32), BLOCK), pl.ds(lane, 256)],
            Rn.at[slot, pl.ds(pl.multiple_of(zr * BLOCK, 32), BLOCK), pl.ds(lane, 256)],
            nb_s.at[rb, h], nb_r.at[slot, zr, lane // 256], dev(xn, y, z, cr),
        )

    def own_copy(zr):
        return rcopy(
            PP.at[pl.ds(pl.multiple_of(ks * CHUNK + (o * 4 + zr) * BLOCK, 32), BLOCK), :],
            Ro.at[pl.ds(pl.multiple_of(zr * BLOCK, 32), BLOCK), :],
            own_s.at[zr], own_r.at[zr], sib,
        )

    @pl.when(is_opp)
    def _():
        @pl.loop(0, 8)
        def _(rb):
            at, left, right = piece(ks, rb)
            PP[at, 0:384] = left
            PP[at, 384:512] = right
            opp_copy(rb, 0).start()
            opp_copy(rb, 1).start()

    @pl.loop(0, 8)
    def _(rb):
        at, left, right = piece(kn, rb)
        PP[at, 0:384] = left
        PP[at, 384:512] = right
        nb_copy(rb, 1, lane_d).start()

    @pl.when(jnp.logical_not(is_opp))
    def _():
        @pl.loop(0, 4)
        def _(zr):
            at, left, right = piece(ks, o * 4 + zr)
            PP[at, 0:384] = left
            PP[at, 384:512] = right
            own_copy(zr).start()

        @pl.loop(0, 4)
        def _(zr):
            at, left, right = piece(ks, c * 4 + zr)
            to = pl.ds(pl.multiple_of(zr * BLOCK, 32), BLOCK)
            Ro[to, 0:384] = left
            Ro[to, 384:512] = right

    @pl.loop(0, 8)
    def _(rb):
        opp_copy(rb, 0).wait_recv()
        at = pl.ds(pl.multiple_of(kn * CHUNK + rb * BLOCK, 32), BLOCK)
        lanes = pl.ds(lane_f, 256)
        got = Ropp[pl.ds(pl.multiple_of(rb * BLOCK, 32), BLOCK), :]
        PP[at, lanes] = (PP[at, lanes].astype(F32) + got.astype(F32)).astype(BF16)
        nb_copy(rb, 0, lane_f).start()

    @pl.loop(0, 4)
    def _(q):
        at = pl.ds(pl.multiple_of(q * ITEM, 128), ITEM)
        wq = jnp.concatenate([W[0, at, :], W[1, at, :], W[2, at, :]], axis=1)
        IG[:, at] = dot_nt(DD[:, 0:384], wq).astype(BF16)

    li = pltpu.make_async_copy(IG.at[mine, :], ig_out.at[:, col_c], loc_sem.at[3])
    li.start()
    si = rcopy(IG.at[theirs, :], ig_out.at[:, col_c], sib_s.at[4], sib_r.at[4], sib)
    si.start()

    def z_copy(b):
        return rcopy(
            Sb.at[pl.ds(pl.multiple_of(b * 80, 16), 80), :],
            Rz.at[z], z_s.at[b], z_r.at[z], dev(x, y, b, c),
        )

    @pl.loop(0, 4)
    def _(zr):
        at = pl.ds(pl.multiple_of(zr * BLOCK, 32), BLOCK)

        @pl.when(is_opp)
        def _():
            own_copy(zr).wait_recv()

        for src in (0, 1):
            for h in (0, 1):
                rcopy(
                    Rn.at[src, at, pl.ds(256 * h, 256)],
                    Rn.at[src, at, pl.ds(256 * h, 256)],
                    nb_s.at[0, 0], nb_r.at[src, zr, h], sib,
                ).wait_recv()
        total = Ro[at, :].astype(F32) + Rn[0, at, :].astype(F32) + Rn[1, at, :].astype(F32)
        Sb[at, :] = total.astype(BF16)
        for s in (0, 1):
            b = zr * 2 + s

            @pl.when(b != z)
            def _():
                z_copy(b).start()

    Rz[z] = Sb[pl.ds(pl.multiple_of(z * 80, 16), 80), :]

    @pl.loop(0, 8)
    def _(k):
        @pl.when(k != z)
        def _():
            rcopy(
                Sb.at[pl.ds(pl.multiple_of(k * 80, 16), 80), :],
                Rz.at[k], z_s.at[k], z_r.at[k], dev(x, y, k, c),
            ).wait_recv()

        T[0:80, :] = T[0:80, :] + Rz[k].astype(F32)

    def y_copy(k):
        yr, lr = zl * 4 + k // 2, k % 2
        return rcopy(U.at[k], Ru.at[y], y_s.at[k], y_r.at[y], dev(x, yr, zh * 2 + lr, c))

    self_k = (y % 4) * 2 + zl
    feeds_self = zl == y // 4
    for k in range(8):
        unit = T[10 * k : 10 * k + 16, :].astype(BF16)
        U[k] = unit
        to_self = feeds_self & (self_k == k)

        @pl.when(to_self)
        def _():
            Ru[y] = unit

        @pl.when(jnp.logical_not(to_self))
        def _():
            y_copy(k).start()

    total = None
    for k in range(8):
        @pl.when(jnp.logical_not(feeds_self & (y == k)))
        def _():
            rcopy(
                U.at[k], Ru.at[k], y_s.at[k], y_r.at[k], dev(x, k, zh * 2 + 1 - zl, c)
            ).wait_recv()

        part = Ru[k].astype(F32)
        total = part if total is None else total + part
    total = total * (1.0 / 512.0)
    for j in range(4):
        wg_out[j] = total[0:10, 128 * j : 128 * j + 128]

    li.wait()
    si.wait()
    sh.wait_send()
    so.wait_send()
    sa.wait_send()
    sd.wait_send()

    @pl.when(active)
    def _():
        g1[0].wait_send()
        g1[1].wait_send()
        for sub, d in ((0, 0), (1, 1), (1, 0), (0, 1)):
            forward(y, 0, d, sub).wait_send()

    for t in range(1, 4):
        sources = ((y + 8 - t) % 8, (y + t) % 8)
        for d in (0, 1):
            s = sources[d]

            @pl.when(s // 4 == c)
            def _():
                for sub in (0, 1):
                    if t < 3 or sub == d:
                        forward(s, t, d, sub).wait_send()

    @pl.loop(0, 8)
    def _(rb):
        nb_copy(rb, 0, lane_f).wait_send()
        nb_copy(rb, 1, lane_d).wait_send()

        @pl.when(is_opp)
        def _():
            opp_copy(rb, 0).wait_send()
            opp_copy(rb, 1).wait_send()

        @pl.when(rb != z)
        def _():
            z_copy(rb).wait_send()

        @pl.when(jnp.logical_not(feeds_self & (self_k == rb)))
        def _():
            y_copy(rb).wait_send()

    @pl.when(jnp.logical_not(is_opp))
    def _():
        @pl.loop(0, 4)
        def _(zr):
            own_copy(zr).wait_send()


def local(hidden, out_grad, weights):
    cosine, sine = rope_tables()
    vmem = pl.BlockSpec(memory_space=pltpu.VMEM)
    anyspace = pl.BlockSpec(memory_space=pl.ANY)
    dma = pltpu.SemaphoreType.DMA
    return pl.pallas_call(
        kernel,
        out_shape=(
            jax.ShapeDtypeStruct(hidden.shape, BF16),
            jax.ShapeDtypeStruct((4, 10, HD), F32),
        ),
        in_specs=[anyspace, anyspace, anyspace, vmem, vmem],
        out_specs=(anyspace, vmem),
        scratch_shapes=[
            pltpu.VMEM((256, HALF), BF16),
            pltpu.VMEM((256, HALF), BF16),
            pltpu.VMEM((4, HALF, HD), BF16),
            pltpu.VMEM((HALF, 256), BF16),
            pltpu.VMEM((HALF, 256), BF16),
            pltpu.VMEM((256, 512), F32),
            pltpu.VMEM((SEQ, 512), F32),
            pltpu.VMEM((256, 512), BF16),
            pltpu.VMEM((HALF, 512), BF16),
            pltpu.VMEM((CHUNK, 256), BF16),
            pltpu.VMEM((2, 640, 512), BF16),
            pltpu.VMEM((640, 512), BF16),
            pltpu.VMEM((640, 512), BF16),
            pltpu.VMEM((8, 80, 512), BF16),
            pltpu.VMEM((96, 512), F32),
            pltpu.VMEM((8, 16, 512), BF16),
            pltpu.VMEM((8, 16, 512), BF16),
            pltpu.VMEM((256, HALF), BF16),
            dma((4,)),
            dma((5,)), dma((5,)),
            dma((2,)), dma((2,)),
            dma((4, 2, 2)), dma((4, 2)),
            dma((8, 2)), dma((8,)),
            dma((8, 2)), dma((2, 4, 2)),
            dma((4,)), dma((4,)),
            dma((8,)), dma((8,)),
            dma((8,)), dma((8,)),
        ],
        compiler_params=pltpu.CompilerParams(
            collective_id=0, has_side_effects=True, vmem_limit_bytes=48 * 1024 * 1024
        ),
    )(hidden, out_grad, weights, cosine, sine)


def solution(mesh):
    placed = (P(("cuts", "chip"), None), P(("cuts", "chip"), None), P(None, "chip", None))
    return jax.shard_map(
        local,
        mesh=mesh,
        in_specs=placed,
        out_specs=(P(("cuts", "chip"), None), P(None, ("cuts", "chip"), None)),
        check_vma=False,
    )
```

time: 356 us -> 103 us (0.29)
  the two profiles are of different devices: /device:TPU:6 before, /device:TPU:152 now
where the time goes in v1:
time: 103 us
  Pallas kernels  95.2 us (92%)
  local copies, waits for them, and re-layouts  6.95 us (7%)
    pallas_call x1, Pallas kernels, local(): pl.pallas_call(kernel, out_shape=(jax.ShapeDtypeStruct(hidden.shape, BF16...  95.2 us
    unnamed x11, local copies, waits for them, and re-layouts  6.33 us

profile of v1, /device:TPU:152, one launch (start us, length us, event | category | flops | bytes accessed | tf_op | source)
XLA Modules:
  0.0 102.8 jit_solution(12388582532804547455)
XLA Ops:
  0.6 0.0 copy-start
  0.6 1.3 %copy-done = bf16[128,5120]{1,0:T(8,128)(2,1)S(1)} copy-done((bf16[128,5120]{1,0:T(8,128)(2,1)S(1)}, bf16[128,5120]{1,0:T(8,128)(2,1)}, u32[]{:S(2)}) %copy-start) | copy-done | bytes 1310744
  1.9 0.0 copy-start.1
  1.9 1.3 %copy-done.1 = bf16[128,5120]{1,0:T(8,128)(2,1)S(1)} copy-done((bf16[128,5120]{1,0:T(8,128)(2,1)S(1)}, bf16[128,5120]{1,0:T(8,128)(2,1)}, u32[]{:S(2)}) %copy-start.1) | copy-done | bytes 1310744
  3.3 0.0 copy-start.2
  3.3 1.0 copy-done.2
  4.2 0.0 copy-start.3
  4.2 0.8 copy-done.3
  5.1 0.0 copy-start.4
  5.1 0.8 copy-done.4
  5.9 95.2 %shard_map.68 = (bf16[128,5120]{1,0:T(8,128)(2,1)S(1)}, f32[4,10,128]{2,1,0:T(8,128)S(1)}) custom-call(bf16[128,5120]{1,0:T(8,128)(2,1)S(1)} %copy-done, bf16[128,5120]{1,0:T(8,128)(2,1)S(1)} %copy-done.1, bf16[4,320,128]{2,1,0:T(8,128)(2,1)S(1)} %copy-done.2, f32[128,128]{1,0:T(8,128)S(1)} %copy-done.4, f32[128,128]{1,0:T(8,128)S(1)} %copy-done.3), custom_call_target="tpu_custom_call" | custom-call | tf_op jit(solution)/shard_map/pallas_call | solution.py:461
  101.1 0.6 copy.7
  101.7 1.1 %copy.9 = bf16[128,5120]{1,0:T(8,128)(2,1)} copy(bf16[128,5120]{1,0:T(8,128)(2,1)S(1)} %get-tuple-element.6) | data formatting | bytes 2621440
Async XLA Ops:
  0.6 1.3 %copy-start = (bf16[128,5120]{1,0:T(8,128)(2,1)S(1)}, bf16[128,5120]{1,0:T(8,128)(2,1)}, u32[]{:S(2)}) copy-start(bf16[128,5120]{1,0:T(8,128)(2,1)} %hid.1) | copy-start | bytes 3932164
  1.9 1.3 %copy-start.1 = (bf16[128,5120]{1,0:T(8,128)(2,1)S(1)}, bf16[128,5120]{1,0:T(8,128)(2,1)}, u32[]{:S(2)}) copy-start(bf16[128,5120]{1,0:T(8,128)(2,1)} %og.1) | copy-start | bytes 3932164
  3.3 1.0 copy-start.2
  4.2 0.8 copy-start.3
  5.1 0.8 copy-start.4

commit v2 on v1

v2 whole, which is shorter than its diff:
```python
import jax
import jax.numpy as jnp
import numpy as np
from jax import lax
from jax.experimental import pallas as pl
from jax.experimental.pallas import tpu as pltpu
from jax.sharding import PartitionSpec as P

MESH = pl.DeviceIdType.MESH
F32 = jnp.float32
BF16 = jnp.bfloat16

HD = 128
SEQ = 128
HALF = 2560
ITEM = 640
CHUNK = 1280
BLOCK = 160
UNITS = 80


def rope_tables():
    half = HD // 2
    rates = 10000.0 ** (-(np.arange(half) * 2.0) / HD)
    angle = np.arange(SEQ)[:, None] * rates[None, :]
    cosine, sine = np.cos(angle), np.sin(angle)
    return np.stack(
        [np.concatenate([cosine, cosine], axis=1), np.concatenate([-sine, sine], axis=1)]
    ).astype(np.float32)


def turn_table():
    order = np.arange(ITEM).reshape(2, 2, 8, 20).transpose(1, 2, 0, 3).reshape(-1)
    table = np.zeros((ITEM, ITEM), np.float32)
    table[np.arange(ITEM), order] = 1.0
    return table


def dot(a, b):
    return jnp.dot(a, b, preferred_element_type=F32)


def dot_nt(a, b):
    return lax.dot_general(a, b, (((1,), (1,)), ((), ())), preferred_element_type=F32)


def kernel(
    hid, og, wts, cs, turn, ig_out, wg_out,
    Hb, Ob, W, HT, HP, OT, CS, TN, acc, accr, DD,
    PX, Ropp, Rn, Ro, Sb, PY, PZ, RY, RZ, Dz, Dy, DxY, DxZ, SY, SZ, Ty, Tz, Uy, Uz, Fy, Fz, IG,
    loc_sem, sib_s, sib_r, g1_s, g1_r, b_s, b_r, cp_s, cp_r, c_s, c_r,
    opp_s, opp_r, nb_s, nb_r, own_s, own_r, ry_s, ry_r, rz_s, rz_r,
    dz_s, dz_r, dy_s, dy_r, dxy_s, dxy_r, dxz_s, dxz_r, fy_s, fy_r, fz_s, fz_r,
):
    ci = lax.axis_index("cuts")
    ch = lax.axis_index("chip")
    x = ci // 8
    zh = (ci // 2) % 4
    c = ci % 2
    y = ch // 2
    zl = ch % 2
    z = zh * 2 + zl
    o = 1 - c

    def dev(x_, y_, z_, c_):
        return (x_ * 8 + (z_ // 2) * 2 + c_, y_ * 2 + z_ % 2)

    def rcopy(src, dst, ss, rs, to):
        return pltpu.make_async_remote_copy(
            src_ref=src, dst_ref=dst, send_sem=ss, recv_sem=rs, device_id=to, device_id_type=MESH
        )

    def when(cond):
        return pl.when(cond)

    def unless(cond):
        return pl.when(jnp.logical_not(cond))

    def rows(start, size, step):
        return pl.ds(pl.multiple_of(start, step), size)

    sib = dev(x, y, z, o)
    yq = y % 4
    active = y // 4 == c
    mine = rows(c * SEQ, SEQ, SEQ)
    theirs = rows(o * SEQ, SEQ, SEQ)
    col_c = rows(c * HALF, HALF, HALF)
    col_o = rows(o * HALF, HALF, HALF)
    yp, ym = (y + 1) % 8, (y + 7) % 8
    zp, zm = (z + 1) % 8, (z + 7) % 8
    xp, xm = (x + 1) % 4, (x + 3) % 4

    lh = pltpu.make_async_copy(hid.at[:, col_c], Hb.at[mine, :], loc_sem.at[0])
    lo = pltpu.make_async_copy(og.at[:, col_c], Ob.at[mine, :], loc_sem.at[1])
    lw = pltpu.make_async_copy(
        wts.at[pl.ds(0, 2)], W.at[pl.ds(0, 2), yq, rows(zl * 320, 320, 64), :], loc_sem.at[2]
    )
    lq = pltpu.make_async_copy(
        wts.at[pl.ds(2, 2), rows(zh * UNITS, UNITS, 16), :],
        W.at[pl.ds(2, 2), yq, rows(zl * 320 + zh * UNITS, UNITS, 16), :],
        loc_sem.at[6],
    )
    lc = pltpu.make_async_copy(cs, CS, loc_sem.at[4])
    lt = pltpu.make_async_copy(turn, TN, loc_sem.at[5])

    @when(active)
    def _():
        lw.start()
        lq.start()

    lh.start()
    lo.start()
    lt.start()
    lc.start()

    bar = pltpu.get_barrier_semaphore()

    def greet(to):
        pl.semaphore_signal(bar, inc=1, device_id=to, device_id_type=MESH)

    for dy in range(1, 8):
        for l in (0, 1):
            greet(dev(x, (y + dy) % 8, zh * 2 + l, c))
    for dz in range(1, 8):
        greet(dev(x, y, (z + dz) % 8, c))
    for dx in (1, 2, 3):
        for cc in (0, 1):
            greet(dev((x + dx) % 4, y, z, cc))
    greet(sib)
    acc[...] = jnp.zeros_like(acc)
    Ty[...] = jnp.zeros_like(Ty)
    Tz[...] = jnp.zeros_like(Tz)
    pl.semaphore_wait(bar, 14 + 7 + 6 + 1)

    def cp_copy(dy):
        at = rows(zh * UNITS, UNITS, 16)
        return rcopy(
            wts.at[pl.ds(2, 2), at, :],
            W.at[pl.ds(2, 2), yq, rows(zl * 320 + zh * UNITS, UNITS, 16), :],
            cp_s.at[dy], cp_r.at[yq], dev(x, (y + dy) % 8, z, c),
        )

    def g1_copy(i, l):
        return rcopy(
            wts.at[pl.ds(0, 2), pl.ds(160 * i, 160), :],
            W.at[pl.ds(0, 2), yq, rows(l * 320 + 160 * i, 160, 32), :],
            g1_s.at[i], g1_r.at[i], dev(x, y, (zp, zm)[i], c),
        )

    @when(active)
    def _():
        g1_copy(0, zl).start()
        g1_copy(1, zl).start()
        for dy in (1, 7, 2, 6, 3, 5, 4):
            cp_copy(dy).start()

    sh = rcopy(hid.at[:, col_o], Hb.at[mine, :], sib_s.at[0], sib_r.at[0], sib)
    so = rcopy(og.at[:, col_o], Ob.at[mine, :], sib_s.at[1], sib_r.at[1], sib)
    sh.start()
    so.start()

    def b_copy(s, t, d, sub):
        r = W.at[sub, s % 4]
        return rcopy(r, r, b_s.at[t, d, sub], b_r.at[s % 4, sub], dev(x, (yp, ym)[d], z, c))

    def c_copy(s, t, d, sub):
        r = W.at[2 + sub, :, rows((s % 2) * 320 + (s // 2) * UNITS, UNITS, 16), :]
        return rcopy(r, r, c_s.at[t, d, sub], c_r.at[s, sub], dev(x, y, (zp, zm)[d], c))

    def project_qk(s):
        at = rows((s % 4) * ITEM, ITEM, 128)
        acc[:, 0:256] += dot(Hb[:, at], jnp.concatenate([W[0, s % 4], W[1, s % 4]], axis=1))

    def transpose(src, dst, q):
        turned = src[:, q * ITEM : (q + 1) * ITEM].T
        for i in range(4):
            zr, cr = (q % 2) * 2 + i // 2, i % 2
            at = (q // 2) * CHUNK + (cr * 4 + zr) * BLOCK
            dst[at : at + BLOCK, :] = turned[i * BLOCK : (i + 1) * BLOCK, :]

    def transpose_turned(xr):
        low = dot_nt(TN[...], Hb[:, xr * CHUNK : xr * CHUNK + ITEM])
        high = dot_nt(TN[...], Hb[:, xr * CHUNK + ITEM : (xr + 1) * CHUNK])
        for g in range(16):
            at = xr * CHUNK + g * UNITS
            both = jnp.concatenate([low[g * 40 : g * 40 + 40], high[g * 40 : g * 40 + 40]], axis=0)
            HP[at : at + UNITS, :] = both.astype(BF16)

    order = ((0, 0), (1, 1), (1, 0), (0, 1))

    @when(active)
    def _():
        lw.wait()
        lq.wait()
        g1_copy(0, 1 - zl).wait_recv()
        g1_copy(1, 1 - zl).wait_recv()
        for sub, d in order:
            b_copy(y, 0, d, sub).start()

    for k in range(4):
        @unless(active & (k == yq))
        def _():
            at = rows(zl * 320 + zh * UNITS, UNITS, 16)
            r = W.at[pl.ds(2, 2), k, at, :]
            rcopy(r, r, cp_s.at[1], cp_r.at[k], dev(x, yp, z, c)).wait_recv()

    for sub, d in order:
        c_copy(z, 0, d, sub).start()

    lh.wait()
    sh.wait_recv()
    for q in range(4):
        transpose(Hb, HT, q)

    @when(active)
    def _():
        project_qk(y)

    for t in range(1, 5):
        ys = ((y + 8 - t) % 8, (y + t) % 8)
        zs = ((z + 8 - t) % 8, (z + t) % 8)
        if t < 4:
            for i in (0, 1):
                for d in (0, 1):
                    s = ys[d]
                    sub = i if d == 0 else 1 - i

                    @when(s // 4 == c)
                    def _():
                        b_copy(s, 0, 0, sub).wait_recv()
                        if t < 3 or sub == d:
                            b_copy(s, t, d, sub).start()

                for d in (0, 1):
                    s = zs[d]
                    sub = i if d == 0 else 1 - i
                    c_copy(s, 0, 0, sub).wait_recv()
                    if t < 3 or sub == d:
                        c_copy(s, t, d, sub).start()

            if t == 1:
                lt.wait()
                transpose_turned(0)
                transpose_turned(1)
            if t == 2:
                lo.wait()
                so.wait_recv()
                for q in range(4):
                    transpose(Ob, OT, q)
            for d in (0, 1):
                s = ys[d]

                @when(s // 4 == c)
                def _():
                    project_qk(s)

        else:
            s = ys[0]

            @when(s // 4 == c)
            def _():
                b_copy(s, 0, 0, 0).wait_recv()
                b_copy(s, 0, 0, 1).wait_recv()
                project_qk(s)

            c_copy(zs[0], 0, 0, 0).wait_recv()
            c_copy(zs[0], 0, 0, 1).wait_recv()

    wv = jnp.concatenate([W[2, k] for k in range(4)], axis=0)
    acc[:, 256:384] = dot(Hb[...], wv)
    wo = jnp.concatenate([W[3, k] for k in range(4)], axis=0)
    acc[:, 384:512] = dot(Ob[...], wo)

    sa = rcopy(acc.at[theirs, :], accr, sib_s.at[2], sib_r.at[2], sib)
    sa.start()
    lc.wait()
    cosine, sine = CS[0], CS[1]

    def rope(v, sgn):
        return v * cosine + pltpu.roll(v, 64, 1) * (sine * sgn)

    scale = 1.0 / np.sqrt(np.float32(HD))
    at_row = lax.broadcasted_iota(jnp.int32, (SEQ, SEQ), 0)
    at_col = lax.broadcasted_iota(jnp.int32, (SEQ, SEQ), 1)
    sa.wait_recv()
    summed = acc[mine, :] + accr[...]
    query = rope(summed[:, 0:128], 1.0).astype(BF16)
    keys = rope(summed[:, 128:256], 1.0).astype(BF16)
    values = summed[:, 256:384].astype(BF16)
    d_attn = summed[:, 384:512].astype(BF16)
    scores = dot_nt(query, keys) * scale
    d_prob = dot_nt(d_attn, values)
    scores = jnp.where(at_col <= at_row, scores, -jnp.inf)
    expo = jnp.exp(scores - jnp.max(scores, axis=1, keepdims=True))
    prob = expo / jnp.sum(expo, axis=1, keepdims=True)
    prob_b = prob.astype(BF16)
    attn = dot(prob_b, values)
    d_score = prob * (d_prob - jnp.sum(prob * d_prob, axis=1, keepdims=True)) * scale
    d_query = rope(dot(d_score.astype(BF16), keys), -1.0)
    d_key = rope(dot(d_score.T.astype(BF16), query), -1.0)
    d_value = dot(prob.T.astype(BF16), d_attn)
    DD[mine, :] = jnp.concatenate([d_query, d_key, d_value, attn], axis=1).astype(BF16)
    sd = rcopy(DD.at[mine, :], DD.at[mine, :], sib_s.at[3], sib_r.at[3], sib)
    sd.start()
    rcopy(DD.at[theirs, :], DD.at[theirs, :], sib_s.at[3], sib_r.at[3], sib).wait_recv()

    dd = (2 * c + 4 - x) % 4
    is_opp = (dd == 1) | (dd == 2)
    plus = dd < 2
    kn = jnp.where((dd == 0) | (dd == 2), 1, 0)
    ks = 1 - kn
    xn = jnp.where(plus, xp, xm)
    slot = jnp.where(plus, 0, 1)
    half_f = jnp.where(plus, 0, 1)
    half_d = 1 - half_f

    def lane(h):
        return pl.ds(pl.multiple_of(h * 128, 128), 128)

    def x_piece(k, rb):
        at = rows(k * CHUNK + rb * BLOCK, BLOCK, 32)
        left = dot(HT[at, :], DD[:, 0:128])
        right = dot(HP[at, :], DD[:, 128:256])
        return jnp.concatenate([left, right], axis=1).astype(BF16)

    def opp_copy(rb, h):
        return rcopy(
            PX.at[rows(ks * CHUNK + rb * BLOCK, BLOCK, 32), lane(h)],
            Ropp.at[rows(rb * BLOCK, BLOCK, 32), :],
            opp_s.at[rb, h], opp_r.at[rb], dev((xp, xm)[h], y, z, c),
        )

    def nb_copy(rb, h):
        cr, zr = rb // 4, rb % 4
        return rcopy(
            PX.at[rows(kn * CHUNK + rb * BLOCK, BLOCK, 32), lane(h)],
            Rn.at[slot, rows(zr * BLOCK, BLOCK, 32), lane(h)],
            nb_s.at[rb, h], nb_r.at[slot, zr, h], dev(xn, y, z, cr),
        )

    def own_copy(zr):
        return rcopy(
            PX.at[rows(ks * CHUNK + (o * 4 + zr) * BLOCK, BLOCK, 32), :],
            Ro.at[rows(zr * BLOCK, BLOCK, 32), :],
            own_s.at[zr], own_r.at[zr], sib,
        )

    def ring(pos, mat, lanes, PR, RR, s_sem, r_sem, to):
        def chunk_of(k, d):
            return (pos + (k if d == 0 else 8 - k)) % 8

        def compute(i):
            lhs = jnp.concatenate(
                [mat[rows(g * 640 + i * UNITS, UNITS, 16), :] for g in range(4)], axis=0
            )
            PR[i] = dot(lhs, DD[:, lanes : lanes + 128]).astype(BF16)

        def copy(k, d):
            i = chunk_of(k, d)
            at = pl.ds(160 * d, 160) if k == 4 else pl.ds(0, 320)
            return rcopy(
                PR.at[i, at, :], RR.at[d, k - 1, at, :], s_sem.at[k - 1, d], r_sem.at[k - 1, d], to[d]
            )

        def step(k):
            for d in (0, 1):
                i = chunk_of(k, d)
                if k == 3:
                    copy(4, d).wait_recv()
                    at = slice(160 * d, 160 * d + 160)
                    PR[i, at, :] = (PR[i, at, :].astype(F32) + RR[d, 3, at, :].astype(F32)).astype(BF16)
                elif k < 3:
                    copy(k + 1, d).wait_recv()
                    PR[i] = (PR[i].astype(F32) + RR[d, k].astype(F32)).astype(BF16)
                copy(k, d).start()

        def finish():
            copy(1, 0).wait_recv()
            copy(1, 1).wait_recv()
            return PR[pos].astype(F32) + RR[0, 0].astype(F32) + RR[1, 0].astype(F32)

        def wait_sends():
            for k in range(1, 5):
                for d in (0, 1):
                    copy(k, d).wait_send()

        def compute_for(k):
            compute(chunk_of(k, 0))
            if k not in (0, 4):
                compute(chunk_of(k, 1))

        return compute_for, step, finish, wait_sends

    y_ring = ring(y, HP, 256, PY, RY, ry_s, ry_r, (dev(x, yp, z, c), dev(x, ym, z, c)))
    z_ring = ring(z, OT, 384, PZ, RZ, rz_s, rz_r, (dev(x, y, zp, c), dev(x, y, zm, c)))

    def dx_copy(S, R, a, cr, s_sem, r_sem):
        return rcopy(
            S.at[pl.ds((a * 2 + cr) * UNITS, UNITS), :], R.at[x],
            s_sem.at[a * 2 + cr], r_sem.at[x], dev(2 * c + a, y, z, cr),
        )

    def dx_send(S, R, s_sem, r_sem):
        for a in (0, 1):
            for cr in (0, 1):
                to_self = (2 * c + a == x) & (cr == c)

                @when(to_self)
                def _():
                    R[x] = S[(a * 2 + cr) * UNITS : (a * 2 + cr + 1) * UNITS, :]

                @unless(to_self)
                def _():
                    dx_copy(S, R, a, cr, s_sem, r_sem).start()

    def dx_receive(R, s_sem, r_sem):
        total = None
        for k in range(4):
            @unless((k == x) & (x // 2 == c))
            def _():
                rcopy(R.at[k], R.at[k], s_sem.at[0], r_sem.at[k], sib).wait_recv()

            total = R[k].astype(F32) if total is None else total + R[k].astype(F32)
        return total

    def dx_wait(S, R, s_sem, r_sem):
        for a in (0, 1):
            for cr in (0, 1):
                @unless((2 * c + a == x) & (cr == c))
                def _():
                    dx_copy(S, R, a, cr, s_sem, r_sem).wait_send()

    def dz_copy(i):
        return rcopy(
            Sb.at[rows(i * UNITS, UNITS, 16), pl.ds(0, 128)], Dz.at[z],
            dz_s.at[i], dz_r.at[z], dev(x, y, i, c),
        )

    def dy_copy(i):
        return rcopy(
            Sb.at[rows(i * UNITS, UNITS, 16), pl.ds(128, 128)], Dy.at[y],
            dy_s.at[i], dy_r.at[y], dev(x, i, z, c),
        )

    def fy_copy(k):
        yr, lr = zl * 4 + k // 2, k % 2
        return rcopy(Uy.at[k], Fy.at[y], fy_s.at[k], fy_r.at[y], dev(x, yr, zh * 2 + lr, c))

    def fz_copy(k):
        return rcopy(Uz.at[k], Fz.at[z], fz_s.at[k], fz_r.at[z], dev(x, y, k, c))

    self_k = yq * 2 + zl
    feeds_self = zl == y // 4

    y_ring[0](4)
    y_ring[1](4)
    z_ring[0](4)
    z_ring[1](4)

    @when(is_opp)
    def _():
        @pl.loop(0, 8)
        def _(rb):
            PX[rows(ks * CHUNK + rb * BLOCK, BLOCK, 32), :] = x_piece(ks, rb)
            opp_copy(rb, 0).start()
            opp_copy(rb, 1).start()

    @unless(is_opp)
    def _():
        @pl.loop(0, 8)
        def _(rb):
            PX[rows(kn * CHUNK + rb * BLOCK, BLOCK, 32), :] = x_piece(kn, rb)
            nb_copy(rb, half_d).start()

    y_ring[0](3)
    y_ring[1](3)
    z_ring[0](3)
    z_ring[1](3)

    @when(is_opp)
    def _():
        @pl.loop(0, 8)
        def _(rb):
            PX[rows(kn * CHUNK + rb * BLOCK, BLOCK, 32), :] = x_piece(kn, rb)
            nb_copy(rb, half_d).start()

    y_ring[0](2)
    y_ring[1](2)
    z_ring[0](2)
    z_ring[1](2)

    @pl.loop(0, 8)
    def _(rb):
        opp_copy(rb, 0).wait_recv()
        at = rows(kn * CHUNK + rb * BLOCK, BLOCK, 32)
        got = Ropp[rows(rb * BLOCK, BLOCK, 32), :]
        PX[at, lane(half_f)] = (PX[at, lane(half_f)].astype(F32) + got.astype(F32)).astype(BF16)
        nb_copy(rb, half_f).start()

    y_ring[0](1)
    y_ring[1](1)
    z_ring[0](1)
    z_ring[1](1)

    @unless(is_opp)
    def _():
        @pl.loop(0, 4)
        def _(zr):
            PX[rows(ks * CHUNK + (o * 4 + zr) * BLOCK, BLOCK, 32), :] = x_piece(ks, o * 4 + zr)
            own_copy(zr).start()

        @pl.loop(0, 4)
        def _(zr):
            Ro[rows(zr * BLOCK, BLOCK, 32), :] = x_piece(ks, c * 4 + zr)

    y_ring[0](0)
    z_ring[0](0)

    @pl.loop(0, 4)
    def _(q):
        wq = jnp.concatenate([W[0, q], W[1, q], W[2, q]], axis=1)
        IG[:, rows(q * ITEM, ITEM, 128)] = dot_nt(DD[:, 0:384], wq).astype(BF16)

    li = pltpu.make_async_copy(IG.at[mine, :], ig_out.at[:, col_c], loc_sem.at[3])
    li.start()
    si = rcopy(IG.at[theirs, :], ig_out.at[:, col_c], sib_s.at[4], sib_r.at[4], sib)
    si.start()

    SY[...] = y_ring[2]().astype(BF16)
    dx_send(SY, DxY, dxy_s, dxy_r)
    SZ[...] = z_ring[2]().astype(BF16)
    dx_send(SZ, DxZ, dxz_s, dxz_r)

    @pl.loop(0, 4)
    def _(zr):
        at = rows(zr * BLOCK, BLOCK, 32)

        @when(is_opp)
        def _():
            own_copy(zr).wait_recv()

        for src in (0, 1):
            for h in (0, 1):
                r = Rn.at[src, at, pl.ds(128 * h, 128)]
                rcopy(r, r, nb_s.at[0, 0], nb_r.at[src, zr, h], sib).wait_recv()
        total = Ro[at, :].astype(F32) + Rn[0, at, :].astype(F32) + Rn[1, at, :].astype(F32)
        Sb[at, :] = total.astype(BF16)
        for s in (0, 1):
            i = zr * 2 + s

            @when(i != z)
            def _():
                dz_copy(i).start()

            @when(i != y)
            def _():
                dy_copy(i).start()

    Dz[z] = Sb[rows(z * UNITS, UNITS, 16), 0:128]
    Dy[y] = Sb[rows(y * UNITS, UNITS, 16), 128:256]
    Ty[0:UNITS, 128:256] = dx_receive(DxZ, dxz_s, dxz_r)
    Tz[0:UNITS, 128:256] = dx_receive(DxY, dxy_s, dxy_r)

    @pl.loop(0, 8)
    def _(k):
        @when(k != z)
        def _():
            rcopy(Dz.at[k], Dz.at[k], dz_s.at[k], dz_r.at[k], dev(x, y, k, c)).wait_recv()

        Ty[0:UNITS, 0:128] = Ty[0:UNITS, 0:128] + Dz[k].astype(F32)

    for k in range(8):
        unit = Ty[10 * k : 10 * k + 16, :].astype(BF16)
        Uy[k] = unit
        to_self = feeds_self & (self_k == k)

        @when(to_self)
        def _():
            Fy[y] = unit

        @unless(to_self)
        def _():
            fy_copy(k).start()

    @pl.loop(0, 8)
    def _(k):
        @when(k != y)
        def _():
            rcopy(Dy.at[k], Dy.at[k], dy_s.at[k], dy_r.at[k], dev(x, k, z, c)).wait_recv()

        Tz[0:UNITS, 0:128] = Tz[0:UNITS, 0:128] + Dy[k].astype(F32)

    for k in range(8):
        unit = Tz[10 * k : 10 * k + 16, :].astype(BF16)
        Uz[k] = unit

        @when(k == z)
        def _():
            Fz[z] = unit

        @when(k != z)
        def _():
            fz_copy(k).start()

    total = None
    for k in range(8):
        @unless(feeds_self & (y == k))
        def _():
            rcopy(Fy.at[k], Fy.at[k], fy_s.at[k], fy_r.at[k], sib).wait_recv()

        total = Fy[k].astype(F32) if total is None else total + Fy[k].astype(F32)
    total = total * (1.0 / 512.0)
    wg_out[0] = total[0:10, 0:128]
    wg_out[3] = total[0:10, 128:256]
    total = None
    for k in range(8):
        @when(z != k)
        def _():
            rcopy(Fz.at[k], Fz.at[k], fz_s.at[k], fz_r.at[k], sib).wait_recv()

        total = Fz[k].astype(F32) if total is None else total + Fz[k].astype(F32)
    total = total * (1.0 / 512.0)
    wg_out[1] = total[0:10, 0:128]
    wg_out[2] = total[0:10, 128:256]

    sh.wait_send()
    so.wait_send()

    @when(active)
    def _():
        g1_copy(0, zl).wait_send()
        g1_copy(1, zl).wait_send()
        for dy in range(1, 8):
            cp_copy(dy).wait_send()
        for sub, d in order:
            b_copy(y, 0, d, sub).wait_send()

    for sub, d in order:
        c_copy(z, 0, d, sub).wait_send()
    for t in range(1, 4):
        for d in (0, 1):
            s = ((y + 8 - t) % 8, (y + t) % 8)[d]
            zs = ((z + 8 - t) % 8, (z + t) % 8)[d]
            for sub in (0, 1):
                if t < 3 or sub == d:
                    c_copy(zs, t, d, sub).wait_send()

                    @when(s // 4 == c)
                    def _():
                        b_copy(s, t, d, sub).wait_send()

    sa.wait_send()
    sd.wait_send()

    li.wait()
    si.wait()
    y_ring[3]()
    z_ring[3]()
    dx_wait(SY, DxY, dxy_s, dxy_r)
    dx_wait(SZ, DxZ, dxz_s, dxz_r)

    @pl.loop(0, 8)
    def _(k):
        nb_copy(k, half_f).wait_send()
        nb_copy(k, half_d).wait_send()

        @when(is_opp)
        def _():
            opp_copy(k, 0).wait_send()
            opp_copy(k, 1).wait_send()

        @when(k != z)
        def _():
            dz_copy(k).wait_send()

        @when(k != y)
        def _():
            dy_copy(k).wait_send()

    @unless(is_opp)
    def _():
        @pl.loop(0, 4)
        def _(zr):
            own_copy(zr).wait_send()

    @pl.loop(0, 8)
    def _(k):
        @when(k != z)
        def _():
            fz_copy(k).wait_send()

        @unless(feeds_self & (self_k == k))
        def _():
            fy_copy(k).wait_send()


def local(hidden, out_grad, weights):
    table = jnp.asarray(rope_tables())
    turn = jnp.asarray(turn_table(), BF16)
    vmem = pl.BlockSpec(memory_space=pltpu.VMEM)
    hbm = pl.BlockSpec(memory_space=pltpu.HBM)
    dma = pltpu.SemaphoreType.DMA
    v = pltpu.VMEM
    return pl.pallas_call(
        kernel,
        out_shape=(
            jax.ShapeDtypeStruct(hidden.shape, BF16),
            jax.ShapeDtypeStruct((4, 10, HD), F32),
        ),
        in_specs=[hbm] * 5,
        out_specs=(hbm, vmem),
        scratch_shapes=[
            v((256, HALF), BF16),
            v((256, HALF), BF16),
            v((4, 4, ITEM, HD), BF16),
            v((HALF, 256), BF16),
            v((HALF, 256), BF16),
            v((HALF, 256), BF16),
            v((2, SEQ, HD), F32),
            v((ITEM, ITEM), BF16),
            v((256, 512), F32),
            v((SEQ, 512), F32),
            v((256, 512), BF16),
            v((HALF, 256), BF16),
            v((CHUNK, 128), BF16),
            v((2, 640, 256), BF16),
            v((640, 256), BF16),
            v((640, 256), BF16),
            v((8, 320, 128), BF16),
            v((8, 320, 128), BF16),
            v((2, 4, 320, 128), BF16),
            v((2, 4, 320, 128), BF16),
            v((8, UNITS, 128), BF16),
            v((8, UNITS, 128), BF16),
            v((4, UNITS, 128), BF16),
            v((4, UNITS, 128), BF16),
            v((320, 128), BF16),
            v((320, 128), BF16),
            v((96, 256), F32),
            v((96, 256), F32),
            v((8, 16, 256), BF16),
            v((8, 16, 256), BF16),
            v((8, 16, 256), BF16),
            v((8, 16, 256), BF16),
            v((256, HALF), BF16),
            dma((7,)), dma((5,)), dma((5,)),
            dma((2,)), dma((2,)),
            dma((4, 2, 2)), dma((4, 2)),
            dma((8,)), dma((4,)),
            dma((4, 2, 2)), dma((8, 2)),
            dma((8, 2)), dma((8,)),
            dma((8, 2)), dma((2, 4, 2)),
            dma((4,)), dma((4,)),
            dma((4, 2)), dma((4, 2)),
            dma((4, 2)), dma((4, 2)),
            dma((8,)), dma((8,)),
            dma((8,)), dma((8,)),
            dma((4,)), dma((4,)),
            dma((4,)), dma((4,)),
            dma((8,)), dma((8,)),
            dma((8,)), dma((8,)),
        ],
        compiler_params=pltpu.CompilerParams(
            collective_id=0, has_side_effects=True, vmem_limit_bytes=62 * 1024 * 1024
        ),
    )(hidden, out_grad, weights, table, turn)


def solution(mesh):
    placed = (P(("cuts", "chip"), None), P(("cuts", "chip"), None), P(None, "chip", None))
    return jax.shard_map(
        local,
        mesh=mesh,
        in_specs=placed,
        out_specs=(P(("cuts", "chip"), None), P(None, ("cuts", "chip"), None)),
        check_vma=False,
    )
```

time: 103 us -> 80.1 us (0.78)
  the two profiles are of different devices: /device:TPU:152 before, /device:TPU:6 now
where the time goes in v2:
time: 80.1 us; the launch traced here: 79.9 us
  Pallas kernels  75.4 us (94%)
  local copies, waits for them, and re-layouts  3.83 us (5%)
    pallas_call x1, Pallas kernels, local(): pl.pallas_call(kernel, out_shape=(jax.ShapeDtypeStruct(hidden.shape, BF16...  75.4 us
    unnamed x1, local copies, waits for them, and re-layouts  2.46 us

profile of v2, /device:TPU:6, one launch (start us, length us, event | category | flops | bytes accessed | tf_op | source)
XLA Modules:
  0.0 79.9 jit_solution(2173277072478887904)
XLA Ops:
  0.6 75.4 %shard_map.68 = (bf16[128,5120]{1,0:T(8,128)(2,1)}, f32[4,10,128]{2,1,0:T(8,128)}) custom-call(bf16[128,5120]{1,0:T(8,128)(2,1)} %hid.1, bf16[128,5120]{1,0:T(8,128)(2,1)} %og.1, bf16[4,320,128]{2,1,0:T(8,128)(2,1)} %wts.1, f32[2,128,128]{2,1,0:T(8,128)} %constant.4.clone.cs, bf16[640,640]{1,0:T(8,128)(2,1)} %constant.5.clone.turn), custom_call_target="tpu_custom_call" | custom-call | tf_op jit(solution)/shard_map/pallas_call | solution.py:704
  76.1 1.4 %copy.7 = f32[4,10,128]{2,0,1:T(4,128)} copy(f32[4,10,128]{2,1,0:T(8,128)} %get-tuple-element.3) | data formatting | bytes 40960 | tf_op jit(solution)/shard_map/pallas_call | solution.py:704
  77.4 2.5 %copy.9 = bf16[128,5120]{1,0:T(8,128)(2,1)} copy(bf16[128,5120]{1,0:T(8,128)(2,1)} %get-tuple-element.6) | data formatting | bytes 2621440

commit v3 on v2

--- a/solution.py
+++ b/solution.py
@@ -452,6 +452,16 @@
     self_k = yq * 2 + zl
     feeds_self = zl == y // 4
 
+    def at_turn(i):
+        return (i % 2) * 4 + i // 2
+
+    def neighbour_pieces():
+        @pl.loop(0, 8)
+        def _(i):
+            rb = at_turn(i)
+            PX[rows(kn * CHUNK + rb * BLOCK, BLOCK, 32), :] = x_piece(kn, rb)
+            nb_copy(rb, half_d).start()
+
     y_ring[0](4)
     y_ring[1](4)
     z_ring[0](4)
@@ -460,17 +470,15 @@
     @when(is_opp)
     def _():
         @pl.loop(0, 8)
-        def _(rb):
+        def _(i):
+            rb = at_turn(i)
             PX[rows(ks * CHUNK + rb * BLOCK, BLOCK, 32), :] = x_piece(ks, rb)
             opp_copy(rb, 0).start()
             opp_copy(rb, 1).start()
 
     @unless(is_opp)
     def _():
-        @pl.loop(0, 8)
-        def _(rb):
-            PX[rows(kn * CHUNK + rb * BLOCK, BLOCK, 32), :] = x_piece(kn, rb)
-            nb_copy(rb, half_d).start()
+        neighbour_pieces()
 
     y_ring[0](3)
     y_ring[1](3)
@@ -479,18 +487,37 @@
 
     @when(is_opp)
     def _():
-        @pl.loop(0, 8)
-        def _(rb):
-            PX[rows(kn * CHUNK + rb * BLOCK, BLOCK, 32), :] = x_piece(kn, rb)
-            nb_copy(rb, half_d).start()
+        neighbour_pieces()
+
+    @unless(is_opp)
+    def _():
+        @pl.loop(0, 4)
+        def _(zr):
+            PX[rows(ks * CHUNK + (o * 4 + zr) * BLOCK, BLOCK, 32), :] = x_piece(ks, o * 4 + zr)
+            own_copy(zr).start()
+
+        @pl.loop(0, 4)
+        def _(zr):
+            Ro[rows(zr * BLOCK, BLOCK, 32), :] = x_piece(ks, c * 4 + zr)
 
     y_ring[0](2)
     y_ring[1](2)
     z_ring[0](2)
     z_ring[1](2)
 
+    @pl.loop(0, 4)
+    def _(q):
+        wq = jnp.concatenate([W[0, q], W[1, q], W[2, q]], axis=1)
+        IG[:, rows(q * ITEM, ITEM, 128)] = dot_nt(DD[:, 0:384], wq).astype(BF16)
+
+    li = pltpu.make_async_copy(IG.at[mine, :], ig_out.at[:, col_c], loc_sem.at[3])
+    li.start()
+    si = rcopy(IG.at[theirs, :], ig_out.at[:, col_c], sib_s.at[4], sib_r.at[4], sib)
+    si.start()
+
     @pl.loop(0, 8)
-    def _(rb):
+    def _(i):
+        rb = at_turn(i)
         opp_copy(rb, 0).wait_recv()
         at = rows(kn * CHUNK + rb * BLOCK, BLOCK, 32)
         got = Ropp[rows(rb * BLOCK, BLOCK, 32), :]
@@ -501,38 +528,10 @@
     y_ring[1](1)
     z_ring[0](1)
     z_ring[1](1)
-
-    @unless(is_opp)
-    def _():
-        @pl.loop(0, 4)
-        def _(zr):
-            PX[rows(ks * CHUNK + (o * 4 + zr) * BLOCK, BLOCK, 32), :] = x_piece(ks, o * 4 + zr)
-            own_copy(zr).start()
-
-        @pl.loop(0, 4)
-        def _(zr):
-            Ro[rows(zr * BLOCK, BLOCK, 32), :] = x_piece(ks, c * 4 + zr)
-
     y_ring[0](0)
     z_ring[0](0)
 
-    @pl.loop(0, 4)
-    def _(q):
-        wq = jnp.concatenate([W[0, q], W[1, q], W[2, q]], axis=1)
-        IG[:, rows(q * ITEM, ITEM, 128)] = dot_nt(DD[:, 0:384], wq).astype(BF16)
-
-    li = pltpu.make_async_copy(IG.at[mine, :], ig_out.at[:, col_c], loc_sem.at[3])
-    li.start()
-    si = rcopy(IG.at[theirs, :], ig_out.at[:, col_c], sib_s.at[4], sib_r.at[4], sib)
-    si.start()
-
-    SY[...] = y_ring[2]().astype(BF16)
-    dx_send(SY, DxY, dxy_s, dxy_r)
-    SZ[...] = z_ring[2]().astype(BF16)
-    dx_send(SZ, DxZ, dxz_s, dxz_r)
-
-    @pl.loop(0, 4)
-    def _(zr):
+    def x_done(zr):
         at = rows(zr * BLOCK, BLOCK, 32)
 
         @when(is_opp)
@@ -556,6 +555,15 @@
             def _():
                 dy_copy(i).start()
 
+    x_done(0)
+    x_done(1)
+    SY[...] = y_ring[2]().astype(BF16)
+    dx_send(SY, DxY, dxy_s, dxy_r)
+    SZ[...] = z_ring[2]().astype(BF16)
+    dx_send(SZ, DxZ, dxz_s, dxz_r)
+    x_done(2)
+    x_done(3)
+
     Dz[z] = Sb[rows(z * UNITS, UNITS, 16), 0:128]
     Dy[y] = Sb[rows(y * UNITS, UNITS, 16), 128:256]
     Ty[0:UNITS, 128:256] = dx_receive(DxZ, dxz_s, dxz_r)
@@ -610,8 +618,8 @@
 
         total = Fy[k].astype(F32) if total is None else total + Fy[k].astype(F32)
     total = total * (1.0 / 512.0)
-    wg_out[0] = total[0:10, 0:128]
-    wg_out[3] = total[0:10, 128:256]
+    wg_out[:, 0, :] = total[0:10, 0:128]
+    wg_out[:, 3, :] = total[0:10, 128:256]
     total = None
     for k in range(8):
         @when(z != k)
@@ -620,8 +628,8 @@
 
         total = Fz[k].astype(F32) if total is None else total + Fz[k].astype(F32)
     total = total * (1.0 / 512.0)
-    wg_out[1] = total[0:10, 0:128]
-    wg_out[2] = total[0:10, 128:256]
+    wg_out[:, 1, :] = total[0:10, 0:128]
+    wg_out[:, 2, :] = total[0:10, 128:256]
 
     sh.wait_send()
     so.wait_send()
@@ -694,6 +702,25 @@
             fy_copy(k).wait_send()
 
 
+def hand_over(ig, wg, ig_out, wg_out, held, held_wg, into, out):
+    def moves(source, target, sem):
+        pairs = [(source[1], target[1], 8)]
+        for k in range(8):
+            at = pl.ds(16 * k, 16)
+            pairs.append((source[0].at[at, :], target[0].at[at, :], k))
+        return [pltpu.make_async_copy(a, b, sem.at[k]) for a, b, k in pairs]
+
+    inward = moves((ig, wg), (held, held_wg), into)
+    outward = moves((held, held_wg), (ig_out, wg_out), out)
+    for move in inward:
+        move.start()
+    for first, second in zip(inward, outward):
+        first.wait()
+        second.start()
+    for move in outward:
+        move.wait()
+
+
 def local(hidden, out_grad, weights):
     table = jnp.asarray(rope_tables())
     turn = jnp.asarray(turn_table(), BF16)
@@ -701,12 +728,13 @@
     hbm = pl.BlockSpec(memory_space=pltpu.HBM)
     dma = pltpu.SemaphoreType.DMA
     v = pltpu.VMEM
-    return pl.pallas_call(
+    results = (
+        jax.ShapeDtypeStruct(hidden.shape, BF16),
+        jax.ShapeDtypeStruct((10, 4, HD), F32),
+    )
+    found = pl.pallas_call(
         kernel,
-        out_shape=(
-            jax.ShapeDtypeStruct(hidden.shape, BF16),
-            jax.ShapeDtypeStruct((4, 10, HD), F32),
-        ),
+        out_shape=results,
         in_specs=[hbm] * 5,
         out_specs=(hbm, vmem),
         scratch_shapes=[
@@ -764,6 +792,14 @@
             collective_id=0, has_side_effects=True, vmem_limit_bytes=62 * 1024 * 1024
         ),
     )(hidden, out_grad, weights, table, turn)
+    input_grad, weight_grads = pl.pallas_call(
+        hand_over,
+        out_shape=results,
+        in_specs=[hbm, hbm],
+        out_specs=(hbm, hbm),
+        scratch_shapes=[v((SEQ, 2 * HALF), BF16), v((10, 4, HD), F32), dma((9,)), dma((9,))],
+    )(*found)
+    return input_grad, jnp.transpose(weight_grads, (1, 0, 2))
 
 
 def solution(mesh):

time: 80.1 us -> 76.9 us (0.960)
  local copies, waits for them, and re-layouts: 3.83 us -> 0 us
    unnamed x1 -> x0, local copies, waits for them, and re-layouts: 2.46 us -> none
    pallas_call x1 -> x0, local copies, waits for them, and re-layouts: 1.37 us -> none  [local(): pl.pallas_call(kernel, out_shape=(jax.ShapeDtypeStruct(hidden.shape, BF16...]
    pallas_call x1 -> x2, Pallas kernels: 75.4 us -> 76.1 us  [the longest x1 73.9 us: local(): pl.pallas_call(kernel, out_shape=results, in_specs=[hbm] * 5, out_specs=(...]
where the time goes in v3:
time: 76.9 us; the launch traced here: 76.8 us
  Pallas kernels  76.1 us (99%)
    pallas_call x1, Pallas kernels, local(): pl.pallas_call(kernel, out_shape=results, in_specs=[hbm] * 5, out_specs=(...  73.9 us
    pallas_call x1, Pallas kernels, local(): pl.pallas_call(hand_over, out_shape=results, in_specs=[hbm, hbm], out_spe...  2.24 us

profile of v3, /device:TPU:6, one launch (start us, length us, event | category | flops | bytes accessed | tf_op | source)
XLA Modules:
  0.0 76.8 jit_solution(1133949319852651467)
XLA Ops:
  0.6 73.9 %shard_map.68 = (bf16[128,5120]{1,0:T(8,128)(2,1)}, f32[10,4,128]{2,1,0:T(4,128)}) custom-call(bf16[128,5120]{1,0:T(8,128)(2,1)} %hid.1, bf16[128,5120]{1,0:T(8,128)(2,1)} %og.1, bf16[4,320,128]{2,1,0:T(8,128)(2,1)} %wts.1, f32[2,128,128]{2,1,0:T(8,128)} %constant.4.clone.cs, bf16[640,640]{1,0:T(8,128)(2,1)} %constant.5.clone.turn), custom_call_target="tpu_custom_call" | custom-call | tf_op jit(solution)/shard_map/pallas_call | solution.py:735
  74.5 2.2 %shard_map.69 = (bf16[128,5120]{1,0:T(8,128)(2,1)}, f32[10,4,128]{2,1,0:T(4,128)}) custom-call(bf16[128,5120]{1,0:T(8,128)(2,1)} %get-tuple-element.6.ig, f32[10,4,128]{2,1,0:T(4,128)} %get-tuple-element.7.wg), custom_call_target="tpu_custom_call" | custom-call | tf_op jit(solution)/shard_map/pallas_call | solution.py:795

commit v4 on v3

--- a/solution.py
+++ b/solution.py
@@ -149,10 +149,10 @@
 
     @when(active)
     def _():
+        for dy in (1, 7, 2, 6, 3, 5, 4):
+            cp_copy(dy).start()
         g1_copy(0, zl).start()
         g1_copy(1, zl).start()
-        for dy in (1, 7, 2, 6, 3, 5, 4):
-            cp_copy(dy).start()
 
     sh = rcopy(hid.at[:, col_o], Hb.at[mine, :], sib_s.at[0], sib_r.at[0], sib)
     so = rcopy(og.at[:, col_o], Ob.at[mine, :], sib_s.at[1], sib_r.at[1], sib)

time: 76.9 us -> 76.9 us (level)
  no operation moved by 1% of the time
where the time goes in v4:
time: 76.9 us; the launch traced here: 76.8 us
  Pallas kernels  76.1 us (99%)
    pallas_call x1, Pallas kernels, local(): pl.pallas_call(kernel, out_shape=results, in_specs=[hbm] * 5, out_specs=(...  73.9 us
    pallas_call x1, Pallas kernels, local(): pl.pallas_call(hand_over, out_shape=results, in_specs=[hbm, hbm], out_spe...  2.24 us

profile of v4, /device:TPU:6, one launch (start us, length us, event | category | flops | bytes accessed | tf_op | source)
XLA Modules:
  0.0 76.8 jit_solution(14391233415023503436)
XLA Ops:
  0.6 73.9 %shard_map.68 = (bf16[128,5120]{1,0:T(8,128)(2,1)}, f32[10,4,128]{2,1,0:T(4,128)}) custom-call(bf16[128,5120]{1,0:T(8,128)(2,1)} %hid.1, bf16[128,5120]{1,0:T(8,128)(2,1)} %og.1, bf16[4,320,128]{2,1,0:T(8,128)(2,1)} %wts.1, f32[2,128,128]{2,1,0:T(8,128)} %constant.4.clone.cs, bf16[640,640]{1,0:T(8,128)(2,1)} %constant.5.clone.turn), custom_call_target="tpu_custom_call" | custom-call | tf_op jit(solution)/shard_map/pallas_call | solution.py:735
  74.5 2.2 %shard_map.69 = (bf16[128,5120]{1,0:T(8,128)(2,1)}, f32[10,4,128]{2,1,0:T(4,128)}) custom-call(bf16[128,5120]{1,0:T(8,128)(2,1)} %get-tuple-element.6.ig, f32[10,4,128]{2,1,0:T(4,128)} %get-tuple-element.7.wg), custom_call_target="tpu_custom_call" | custom-call | tf_op jit(solution)/shard_map/pallas_call | solution.py:795
